TPU v7x, 256 devices: a whole 4x4x8 slice. The times are simulated.
256 devices in a mesh: ctx: 32 (over y, z), heads: 8 (over x, core).
Axes of the slice: x: 4, y: 4, z: 8, core: 2. Of those that a mesh axis runs over, the one named last changes fastest.
Arguments:
- mixer_input: bfloat16 [32768, 6144], P('ctx', 'heads'), parts along dimension 1, may hold values from -6 to 6
- conv_weight: float32 [4, 6144], P(None, 'heads'), parts along dimension 1, may hold values from -3 to 3
- log_decay: float32 [64, 32768], P('heads', 'ctx'), parts along dimension 0, may hold values from -1 to 0
- level_weight: float32 [7, 64, 32768], P(None, 'heads', 'ctx'), parts along dimension 1, may hold values from 0.2 to 2
- norm_gain: float32 [4096], P('heads'), parts along dimension 0, may hold values from 0.5 to 1.5
Outputs:
- normed_output: bfloat16 [32768, 4096], P('ctx', 'heads'), parts along dimension 1
There are 8 independent parts, one for each index of `heads`. A program takes and returns all parts, laid end to end along the dimension named above; each array names one. Nothing has to cross between parts.
All inputs are finite; a program needn't handle non-finite values.
Results may differ from a plain program's by a relative error of at most 0.0075.
Values may be sent and summed in bfloat16 or wider, within the bound.
A program may use at most 128 MiB of HBM per device.

v0:
```python
import jax
import jax.numpy as jnp
from jax import lax
from jax.sharding import PartitionSpec as P

HEADS_PART = 8
HEAD_DIM = 64
STATE = 128
STRETCH = 256
WIDTH_G = 512


def passed_along(block, axis, distance):
    devices = range(lax.axis_size(axis))
    route = [(i - distance, i) for i in devices if i - distance in devices]
    return lax.ppermute(block, axis, route)


def convolve(mixer_input, rim_rows, conv_weight):
    padded = jnp.concatenate([rim_rows, mixer_input], axis=0)
    row_count = mixer_input.shape[0]
    running = jnp.zeros(mixer_input.shape, jnp.float32)
    for tap_row in range(conv_weight.shape[0]):
        running = running + conv_weight[tap_row] * padded[tap_row : tap_row + row_count]
    return jax.nn.silu(running).astype(jnp.bfloat16)


def shard_terms(activated, log_decay, level_weight):
    row_count = activated.shape[0]
    stretches = row_count // STRETCH
    inputs_all = activated[:, :WIDTH_G].reshape(stretches, STRETCH, HEADS_PART, HEAD_DIM)
    keys_all = activated[:, WIDTH_G : WIDTH_G + STATE].reshape(stretches, STRETCH, STATE)
    query_all = activated[:, WIDTH_G + STATE :].reshape(stretches, STRETCH, STATE)
    rate_all = log_decay.reshape(HEADS_PART, stretches, STRETCH).transpose(1, 0, 2)
    weight_all = level_weight[:2].reshape(2, HEADS_PART, stretches, STRETCH).transpose(2, 0, 1, 3)
    causal = jnp.arange(STRETCH)[:, None] >= jnp.arange(STRETCH)[None, :]

    def one_stretch(pieces):
        stretch_in, stretch_keys, stretch_query, stretch_rate, stretch_weight = pieces
        inner_sum = jnp.cumsum(stretch_rate, axis=1)
        scores = jnp.dot(stretch_query, stretch_keys.T, preferred_element_type=jnp.float32)
        decay_gap = inner_sum[:, :, None] - inner_sum[:, None, :]
        decay_map = jnp.exp(jnp.where(causal[None], decay_gap, -jnp.inf))
        mixing = (stretch_weight[0][:, :, None] * decay_map * scores[None]).astype(jnp.bfloat16)
        own_stretch = jnp.einsum(
            "hqk,khp->qhp", mixing, stretch_in, preferred_element_type=jnp.float32
        )
        to_end = jnp.exp(inner_sum[:, -1:] - inner_sum)
        scaled = (to_end[:, :, None] * stretch_keys[None]).astype(jnp.bfloat16)
        stretch_state = jnp.einsum(
            "hqn,qhp->nhp", scaled, stretch_in, preferred_element_type=jnp.float32
        )
        return (own_stretch, stretch_state, inner_sum)

    own_all, state_all, inner_all = lax.map(
        one_stretch, (inputs_all, keys_all, query_all, rate_all, weight_all)
    )
    totals = inner_all[:, :, -1]

    def carry_step(carried, pieces):
        stretch_state, stretch_total = pieces
        return (jnp.exp(stretch_total)[None, :, None] * carried + stretch_state, carried)

    shard_end, starts = lax.scan(
        carry_step, jnp.zeros((STATE, HEADS_PART, HEAD_DIM), jnp.float32), (state_all, totals)
    )
    readout = jnp.einsum(
        "cqn,cnhp->cqhp", query_all, starts.astype(jnp.bfloat16), preferred_element_type=jnp.float32
    )
    inner_rows = inner_all.transpose(0, 2, 1)
    near_scale = weight_all[:, 1].transpose(0, 2, 1) * jnp.exp(inner_rows)
    mixture = own_all + near_scale[..., None] * readout
    offset = jnp.cumsum(totals, axis=0) - totals
    from_start = jnp.exp(offset[:, None, :] + inner_rows).reshape(row_count, HEADS_PART)
    return (
        mixture.reshape(row_count, WIDTH_G),
        shard_end.reshape(STATE, WIDTH_G),
        jnp.sum(totals, axis=0),
        from_start,
    )


def fenwick_buckets(every_end, every_span, reader, bit_count):
    shards = every_end.shape[0]
    before_all = jnp.cumsum(every_span, axis=0) - every_span
    start_at = lax.dynamic_index_in_dim(before_all, reader, 0, keepdims=False)
    decay_gap = start_at[None, :] - before_all - every_span
    source = jnp.arange(shards, dtype=jnp.int32)
    grouped = every_end.reshape(shards, STATE, HEADS_PART, HEAD_DIM)
    buckets = []
    for level_num in range(bit_count):
        member = (source // 2**level_num == reader // 2**level_num - 1) & (
            reader // 2**level_num % 2 == 1
        )
        factor = jnp.exp(jnp.where(member[:, None], decay_gap, -jnp.inf))
        bucket = jnp.einsum("sh,snhp->nhp", factor, grouped, precision=lax.Precision.HIGHEST)
        buckets.append(bucket.reshape(STATE, WIDTH_G))
    return buckets


def read_levels(queries, buckets, level_weight, from_start):
    row_count = queries.shape[0]
    running = jnp.zeros((row_count, HEADS_PART, HEAD_DIM), jnp.float32)
    for level_num, bucket in enumerate(buckets):
        readout = jnp.dot(queries, bucket.astype(jnp.bfloat16), preferred_element_type=jnp.float32)
        running = running + level_weight[2 + level_num].T[:, :, None] * readout.reshape(
            row_count, HEADS_PART, HEAD_DIM
        )
    return (running * from_start[:, :, None]).reshape(row_count, WIDTH_G)


def normalize(mixture, norm_gain):
    mean_square = jnp.mean(mixture * mixture, axis=1, keepdims=True)
    return (mixture * lax.rsqrt(mean_square + 1e-05) * norm_gain).astype(jnp.bfloat16)


def per_device(mixer_input, conv_weight, log_decay, level_weight, norm_gain):
    tail_rows = mixer_input[mixer_input.shape[0] - (conv_weight.shape[0] - 1) :]
    rim_rows = passed_along(tail_rows, "ctx", 1)
    activated = convolve(mixer_input, rim_rows, conv_weight)
    mixture, shard_end, shard_total, from_start = shard_terms(activated, log_decay, level_weight)
    shard_index = lax.axis_index("ctx")
    bit_count = lax.axis_size("ctx").bit_length() - 1
    every_end, every_span = (
        lax.all_gather(shard_end[None].astype(jnp.bfloat16), "ctx", axis=0, tiled=True).astype(
            jnp.float32
        ),
        lax.all_gather(shard_total[None].astype(jnp.bfloat16), "ctx", axis=0, tiled=True).astype(
            jnp.float32
        ),
    )
    buckets = fenwick_buckets(every_end, every_span, shard_index, bit_count)
    queries = activated[:, WIDTH_G + STATE :]
    mixture = mixture + read_levels(queries, buckets, level_weight, from_start)
    return normalize(mixture, norm_gain)


def solution(mesh):
    placed = (
        P("ctx", "heads"),
        P(None, "heads"),
        P("heads", "ctx"),
        P(None, "heads", "ctx"),
        P("heads"),
    )
    return jax.shard_map(
        per_device, mesh=mesh, in_specs=placed, out_specs=P("ctx", "heads"), check_vma=False
    )
```

profile of v0, /device:TPU:2, one launch (start us, length us, event | category | flops | bytes accessed | tf_op | source)
XLA Modules:
  0.0 174.4 jit_solution(11665792653411755729)
XLA Ops:
  7.3 3.8 %collective-permute-start = (bf16[3,768]{1,0:T(4,128)(2,1)S(1)}, bf16[3,768]{1,0:T(4,128)(2,1)S(1)}, u32[]{:S(2)}, u32[]{:S(2)}) collective-permute-start(bf16[3,768]{1,0:T(4,128)(2,1)S(1)} %slice.74), channel_id=1, source_target_pairs={{0,8},{8,16},{16,24},{24,32},{32,40},{40,48},{48,56},{56,64},{64,7... | collective-permute-start | bytes 13832 | tf_op jit(solution)/shard_map/ppermute | solution.py:16
  12.4 4.5 %multiply_convert_fusion.4 = bf16[1024,768]{1,0:T(8,128)(2,1)S(1)} fusion(bf16[1024,768]{1,0:T(8,128)(2,1)} %param.9, bf16[3,768]{1,0:T(4,128)(2,1)S(1)} %collective-permute-done, f32[768]{0:T(1024)S(1)} %get-tuple-element.195, f32[768]{0:T(1024)S(1)} %get-tuple-element.196, f32[768]{0:T(1024)S(1)} %get-tuple-element.194, f32[768]{0:T(1024)S(1)} %get-tuple-element.193), kind=kLoop, calls=%fused_computation.54 | loop fusion | flops 19660800 | bytes 3162624 | tf_op jit(solution)/shard_map/convert_element_type | solution.py:25
  17.7 2.1 %reshape.288 = bf16[4,256,8,64]{3,2,1,0:T(8,128)(2,1)} reshape(bf16[1024,512]{1,0:T(8,128)(2,1)S(1)} %slice.104) | data formatting | bytes 2097152 | tf_op jit(solution)/shard_map/reshape | solution.py:31
  19.9 3.1 %copy.37 = bf16[4,256,8,64]{1,3,2,0:T(8,128)(2,1)} copy(bf16[4,256,8,64]{3,2,1,0:T(8,128)(2,1)} %reshape.288) | data formatting | bytes 2097152
  22.9 28.2 %while.28 = (s32[]{:T(128)}, f32[4,256,8,64]{1,3,2,0:T(8,128)}, f32[4,128,8,64]{1,3,2,0:T(8,128)}, f32[4,8,256]{2,1,0:T(8,128)S(1)}, bf16[4,256,8,64]{1,3,2,0:T(...) while((s32[]{:T(128)}, f32[4,256,8,64]{1,3,2,0:T(8,128)}, ...), condition=%wide.region_3.4_spmd.clone, body=%wide.region_0.3_spmd.clone.sunk | while | flops 120950808 | bytes 2593477 | solution.py:55
  24.7 2.7 %fusion.82 = f32[4,256,8,64]{1,3,2,0:T(8,128)} fusion(f32[4,256,8,64]{1,3,2,0:T(8,128)} %get-tuple-element.344, s32[]{:T(128)} %get-tuple-element.343, f32[256,256]{1,0:T(8,128)S(1)} %fusion.81, f32[8,256]{1,0:T(8,128)S(1)} %add_bitcast_fusion.2, f32[8,256]{1,0:T(8,128)S(1)} %slice_bitcast_fusion.8, pred[256,256]{1,0:T(8,128)(4,1)S(1)} %iota_compare_fusion.2, ...), kind=kOutput, calls=%fused_computation.9.clone.1 | convolution fusion | flops 69730304 | bytes 1139712 | tf_op jit(solution)/shard_map/while/body/eval_jaxpr/hqk,khp->qhp/dot_general | solution.py:45
  27.8 2.2 %fusion.83 = f32[4,128,8,64]{1,3,2,0:T(8,128)} fusion(f32[4,128,8,64]{1,3,2,0:T(8,128)} %get-tuple-element.345, s32[]{:T(128)} %get-tuple-element.343, f32[256,128]{1,0:T(8,128)S(1)} %bitcast_convert_fusion.2, f32[8,256]{1,0:T(8,128)S(1)} %subtract_exponential_fusion.2, bf16[4,256,8,64]{1,3,2,0:T(8,128)(2,1)} %get-tuple-element.358), kind=kOutput, calls=%fused_computation.11.clone.1 | convolution fusion | flops 34078720 | bytes 664576 | tf_op jit(solution)/shard_map/while/body/eval_jaxpr/hqn,qhp->nhp/dot_general | solution.py:50
  31.8 2.7 %fusion.82 = f32[4,256,8,64]{1,3,2,0:T(8,128)} fusion(f32[4,256,8,64]{1,3,2,0:T(8,128)} %get-tuple-element.344, s32[]{:T(128)} %get-tuple-element.343, f32[256,256]{1,0:T(8,128)S(1)} %fusion.81, f32[8,256]{1,0:T(8,128)S(1)} %add_bitcast_fusion.2, f32[8,256]{1,0:T(8,128)S(1)} %slice_bitcast_fusion.8, pred[256,256]{1,0:T(8,128)(4,1)S(1)} %iota_compare_fusion.2, ...), kind=kOutput, calls=%fused_computation.9.clone.1 | convolution fusion | flops 69730304 | bytes 1139712 | tf_op jit(solution)/shard_map/while/body/eval_jaxpr/hqk,khp->qhp/dot_general | solution.py:45
  34.8 2.2 %fusion.83 = f32[4,128,8,64]{1,3,2,0:T(8,128)} fusion(f32[4,128,8,64]{1,3,2,0:T(8,128)} %get-tuple-element.345, s32[]{:T(128)} %get-tuple-element.343, f32[256,128]{1,0:T(8,128)S(1)} %bitcast_convert_fusion.2, f32[8,256]{1,0:T(8,128)S(1)} %subtract_exponential_fusion.2, bf16[4,256,8,64]{1,3,2,0:T(8,128)(2,1)} %get-tuple-element.358), kind=kOutput, calls=%fused_computation.11.clone.1 | convolution fusion | flops 34078720 | bytes 664576 | tf_op jit(solution)/shard_map/while/body/eval_jaxpr/hqn,qhp->nhp/dot_general | solution.py:50
  38.9 2.7 %fusion.82 = f32[4,256,8,64]{1,3,2,0:T(8,128)} fusion(f32[4,256,8,64]{1,3,2,0:T(8,128)} %get-tuple-element.344, s32[]{:T(128)} %get-tuple-element.343, f32[256,256]{1,0:T(8,128)S(1)} %fusion.81, f32[8,256]{1,0:T(8,128)S(1)} %add_bitcast_fusion.2, f32[8,256]{1,0:T(8,128)S(1)} %slice_bitcast_fusion.8, pred[256,256]{1,0:T(8,128)(4,1)S(1)} %iota_compare_fusion.2, ...), kind=kOutput, calls=%fused_computation.9.clone.1 | convolution fusion | flops 69730304 | bytes 1139712 | tf_op jit(solution)/shard_map/while/body/eval_jaxpr/hqk,khp->qhp/dot_general | solution.py:45
  41.8 2.2 %fusion.83 = f32[4,128,8,64]{1,3,2,0:T(8,128)} fusion(f32[4,128,8,64]{1,3,2,0:T(8,128)} %get-tuple-element.345, s32[]{:T(128)} %get-tuple-element.343, f32[256,128]{1,0:T(8,128)S(1)} %bitcast_convert_fusion.2, f32[8,256]{1,0:T(8,128)S(1)} %subtract_exponential_fusion.2, bf16[4,256,8,64]{1,3,2,0:T(8,128)(2,1)} %get-tuple-element.358), kind=kOutput, calls=%fused_computation.11.clone.1 | convolution fusion | flops 34078720 | bytes 664576 | tf_op jit(solution)/shard_map/while/body/eval_jaxpr/hqn,qhp->nhp/dot_general | solution.py:50
  45.9 2.7 %fusion.82 = f32[4,256,8,64]{1,3,2,0:T(8,128)} fusion(f32[4,256,8,64]{1,3,2,0:T(8,128)} %get-tuple-element.344, s32[]{:T(128)} %get-tuple-element.343, f32[256,256]{1,0:T(8,128)S(1)} %fusion.81, f32[8,256]{1,0:T(8,128)S(1)} %add_bitcast_fusion.2, f32[8,256]{1,0:T(8,128)S(1)} %slice_bitcast_fusion.8, pred[256,256]{1,0:T(8,128)(4,1)S(1)} %iota_compare_fusion.2, ...), kind=kOutput, calls=%fused_computation.9.clone.1 | convolution fusion | flops 69730304 | bytes 1139712 | tf_op jit(solution)/shard_map/while/body/eval_jaxpr/hqk,khp->qhp/dot_general | solution.py:45
  48.9 2.2 %fusion.83 = f32[4,128,8,64]{1,3,2,0:T(8,128)} fusion(f32[4,128,8,64]{1,3,2,0:T(8,128)} %get-tuple-element.345, s32[]{:T(128)} %get-tuple-element.343, f32[256,128]{1,0:T(8,128)S(1)} %bitcast_convert_fusion.2, f32[8,256]{1,0:T(8,128)S(1)} %subtract_exponential_fusion.2, bf16[4,256,8,64]{1,3,2,0:T(8,128)(2,1)} %get-tuple-element.358), kind=kOutput, calls=%fused_computation.11.clone.1 | convolution fusion | flops 34078720 | bytes 664576 | tf_op jit(solution)/shard_map/while/body/eval_jaxpr/hqn,qhp->nhp/dot_general | solution.py:50
  51.3 8.5 %while.29 = (s32[]{:T(128)}, f32[128,8,64]{2,1,0:T(8,128)S(1)}, bf16[4,128,8,64]{3,2,1,0:T(8,128)(2,1)}, f32[4,8]{1,0:T(4,128)S(1)}, f32[4,128,8,64]{1,3,2,0:T(8,128)}, /*index=5*/s32[]{:T(128)}, s32[]{:T(128)}) while((s32[]{:T(128)}, f32[128,8,64]{2,1,0:T(8,128)S(1)}, bf16[4,128,8,64]{3,2,1,0:T(8,128)(2,1)}, ...), condition=%wide.region_5.6_spmd.clone, body=%wide.region_4.5_spmd.clone.sunk | while | flops 262147 | bytes 2360000 | solution.py:64
  56.4 1.0 constant_dynamic-slice_fusion.3
  58.5 1.0 constant_dynamic-slice_fusion.3
  62.5 79.0 %all-reduce = bf16[256]{0:T(256)(128)(2,1)S(1)} all-reduce(bf16[256]{0:T(256)(128)(2,1)S(1)} %dynamic-update-slice), channel_id=2, replica_groups=mesh['ctx'=32,'heads'=8] {'ctx'}, use_global_device_ids=true, to_apply=%add | all-reduce | flops 256 | bytes 1024
  141.8 1.8 %copy.40 = bf16[4,128,8,64]{1,3,2,0:T(8,128)(2,1)S(1)} copy(bf16[4,128,8,64]{3,2,1,0:T(8,128)(2,1)} %get-tuple-element.90) | data formatting | bytes 1048576 | tf_op jit(solution)/shard_map/convert_element_type | solution.py:68
  143.8 1.7 fusion.66
  145.5 2.0 %all-gather.3.cloned.1.call-done = bf16[32,128,512]{2,1,0:T(8,128)(2,1)} async-done(((bf16[1,128,512]{2,1,0:T(8,128)(2,1)}), bf16[32,128,512]{2,1,0:T(8,128)(2,1)}) %all-gather.3.cloned.1.call-update) | async-done | bytes 4194320 | tf_op jit(solution)/shard_map/all_gather | solution.py:125
  147.5 6.4 %copy.79 = bf16[32,128,512]{1,2,0:T(8,128)(2,1)} copy(bf16[32,128,512]{2,1,0:T(8,128)(2,1)} %all-gather.3.cloned.1.call-done) | data formatting | bytes 8388608
  153.9 5.2 %fusion.31 = (bf16[8,128,64]{1,2,0:T(8,128)(2,1)S(1)}, bf16[8,128,64]{1,2,0:T(8,128)(2,1)S(1)}, bf16[8,128,64]{1,2,0:T(8,128)(2,1)S(1)}, bf16[8,128,64]{1,2,0:T(8,128)(2,1)S(1)}, bf16[8,128,64]{1,2,0:T(8,128)(2,1)S(1)}) fusion(bf16[8,32,128,64]{2,3,0,1:T(8,128)(2,1)} %bitcast.224, f32[8,32]{0,1:T(8,128)S(1)} %get-tuple-element.241, ...), kind=kLoop, calls=%fused_computation.53 | loop fusion | flops 22740992 | bytes 4854784 | tf_op jit(solution)/shard_map/sh,snhp->nhp/dot_general | solution.py:96
  163.9 1.4 copy.41
  166.2 1.3 copy.46
  (129 shorter events, 25.8 us)
Async XLA Ops:
  6.5 141.0 %all-gather.3.cloned.1.call-start = ((), (), s32[]{:S(2)}) async-start(), calls=%async_computation | async-start | bytes 4325376 | tf_op jit(solution)/shard_map/all_gather | solution.py:125
  7.3 5.1 %collective-permute-start = (bf16[3,768]{1,0:T(4,128)(2,1)S(1)}, bf16[3,768]{1,0:T(4,128)(2,1)S(1)}, u32[]{:S(2)}, u32[]{:S(2)}) collective-permute-start(bf16[3,768]{1,0:T(4,128)(2,1)S(1)} %slice.74), channel_id=1, source_target_pairs={{0,8},{8,16},{16,24},{24,32},{32,40},{40,48},{48,56},{56,64},{64,7... | collective-permute-start | bytes 13832 | tf_op jit(solution)/shard_map/ppermute | solution.py:16
  19.9 3.1 %copy-start.1 = (bf16[1024,128]{1,0:T(8,128)(2,1)S(1)}, bf16[1024,128]{1,0:T(8,128)(2,1)}, u32[]{:S(2)}) copy-start(bf16[1024,128]{1,0:T(8,128)(2,1)} %get-tuple-element.230) | copy-start | bytes 786436
  19.9 3.1 %slice-start = ((f32[7,8,1024]{2,1,0:T(8,128)}), f32[2,8,1024]{2,1,0:T(8,128)S(1)}, s32[]{:S(2)}) async-start(f32[7,8,1024]{2,1,0:T(8,128)} %param.12), calls=%async_computation.1 | async-start | bytes 131072 | tf_op jit(solution)/shard_map/slice | solution.py:35
  51.3 9.6 %copy-start.5 = (u32[256]{0:T(256)S(1)}, u32[256]{0:T(256)}, u32[]{:S(2)}) copy-start(u32[256]{0:T(256)} %constant.212) | copy-start | bytes 3076
  51.3 10.9 %copy-start.3 = (f32[7,8,1024]{2,1,0:T(8,128)S(1)}, f32[7,8,1024]{2,1,0:T(8,128)}, u32[]{:S(2)}) copy-start(f32[7,8,1024]{2,1,0:T(8,128)} %param.12) | copy-start | bytes 688132
  160.9 1.6 copy-start
  160.9 2.2 %copy-start.2 = (f32[4,256,8,64]{1,3,2,0:T(8,128)S(1)}, f32[4,256,8,64]{1,3,2,0:T(8,128)}, u32[]{:S(2)}) copy-start(f32[4,256,8,64]{1,3,2,0:T(8,128)} %get-tuple-element.87) | copy-start | bytes 6291460
  165.2 0.7 copy-start.4
Sparse Core Ops, SparseCore 0:
  60.9 86.5 all-gather.2
where the time goes:
time: 175 us; the launch traced here: 174 us
  blocking collectives  79 us (45%)
  local copies, waits for them, and re-layouts  31.4 us (18%)
  matrix products  24.7 us (14%)
  other arithmetic  18.4 us (11%)
  between operations  14.4 us (8%)
  starting transfers between devices  3.81 us (2%)
  waiting for transfers between devices  2.36 us (1%)
    unnamed x1, blocking collectives  79 us
    unnamed x19, local copies, waits for them, and re-layouts  12.3 us
    dot_general x4, matrix products, one_stretch(): jnp.einsum('hqk,khp->qhp', mixing, stretch_in, preferred_element_type=jnp...  10.9 us
    dot_general x4, matrix products, one_stretch(): jnp.einsum('hqn,qhp->nhp', scaled, stretch_in, preferred_element_type=jnp...  8.65 us
    dot_general x1, other arithmetic, fenwick_buckets(): jnp.einsum('sh,snhp->nhp', factor, grouped, precision=lax.Precision.HIGHEST)  5.24 us
    dynamic_slice x8, local copies, waits for them, and re-layouts, shard_terms(): lax.scan(carry_step, jnp.zeros((STATE, HEADS_PART, HEAD_DIM), jnp.float32...  4.81 us
    convert_element_type x1, other arithmetic, convolve(): return jax.nn.silu(running).astype(jnp.bfloat16)  4.52 us
    ppermute x1, starting transfers between devices, passed_along(): return lax.ppermute(block, axis, route)  3.81 us
  transfers between devices with their start and end apart: 2, of which 2 were waited for; matrix products, arithmetic and copies ran while one was open for 3% of the time, Pallas kernels for 0%

commit v1 on v0

v1 whole, which is shorter than its diff:
```python
import functools

import jax
import jax.numpy as jnp
from jax import lax
from jax.experimental import pallas as pl
from jax.experimental.pallas import tpu as pltpu
from jax.sharding import PartitionSpec as P

HEADS = 8
HEAD_DIM = 64
STATE = 128
STRETCH = 256
WIDTH = 512
TOKENS = 1024
PIECES = TOKENS // STRETCH
SHARDS = 32
BITS = 5
HALF = 128
ROWS = WIDTH // SHARDS
LOG2E = 1.4426950408889634

NT = (((1,), (1,)), ((), ()))
F32 = jnp.float32
BF16 = jnp.bfloat16


def popcount(r):
    count = r % 2
    for k in range(1, BITS):
        count = count + (r // 2**k) % 2
    return count


def activate(window, conv_ref, cols):
    total = conv_ref[3:4, cols] * window[16:144]
    for j in range(3):
        total = total + conv_ref[j : j + 1, cols] * window[13 + j : 141 + j]
    half = 0.5 * total
    return (half + half * jnp.tanh(half)).astype(BF16)


def kernel(
    x_ref, conv_ref, rate_ref, level_ref, gain_ref, out_ref,
    halo, xt, keys, qt, inner, column, state, low, mixed, gain_col, slot_weight,
    send1, recv1, own_span, spans, stage, recv3,
    halo_sem, p1_send, p1_recv, span_send, span_recv, p3_send, p3_recv,
):
    me = lax.axis_index("ctx")
    bits = popcount(me)

    barrier = pltpu.get_barrier_semaphore()
    recv3[...] = jnp.zeros_like(recv3)

    def greet(d, _):
        other = lax.rem(me + d, SHARDS)
        pl.semaphore_signal(barrier, inc=1, device_id={"ctx": other})
        return 0

    lax.fori_loop(1, SHARDS, greet, 0)

    rows = lax.broadcasted_iota(jnp.int32, (STRETCH, STRETCH), 0)
    cols = lax.broadcasted_iota(jnp.int32, (STRETCH, STRETCH), 1)
    lower = jnp.where(rows >= cols, 1.0, 0.0).astype(F32)
    span = jnp.zeros((HEADS, HALF), F32)
    for c in range(PIECES):
        rate = rate_ref[:, c * STRETCH : (c + 1) * STRETCH] * LOG2E
        inner[c] = lax.dot_general(
            rate, lower, NT, precision=lax.Precision.HIGHEST, preferred_element_type=F32
        )
        column[c] = lax.dot_general(
            lower, rate, NT, precision=lax.Precision.HIGHEST, preferred_element_type=F32
        )
        span = span + jnp.broadcast_to(inner[c, :, STRETCH - 1 :], (HEADS, HALF))
    own_span[...] = span

    diag = (rows == cols)[:HALF, :HALF]
    for g in range(WIDTH // HALF):
        row = jnp.broadcast_to(gain_ref[:, g * HALF : (g + 1) * HALF], (HALF, HALF))
        gain_col[g * HALF : (g + 1) * HALF] = jnp.sum(
            jnp.where(diag, row, 0.0), axis=1, keepdims=True
        )

    def place(b, group, act):
        c, half = b // 2, b % 2
        if group < 4:
            xt[c, half, group * HALF : (group + 1) * HALF] = act.T
        elif group == 4:
            keys[c, pl.ds(pl.multiple_of(half * HALF, HALF), HALF)] = act
        else:
            qt[c, half] = act.T

    def block(i, _):
        b = TOKENS // HALF - 1 - i
        start = pl.multiple_of(b * HALF - 16, 16)
        for group in range(6):
            chans = slice(group * HALF, (group + 1) * HALF)
            window = x_ref[pl.ds(start, HALF + 16), chans].astype(F32)
            place(b, group, activate(window, conv_ref, chans))
        return 0

    lax.fori_loop(0, TOKENS // HALF - 1, block, 0)

    pl.semaphore_wait(barrier, SHARDS - 1)
    to_next = pltpu.make_async_remote_copy(
        src_ref=x_ref.at[pl.ds(TOKENS - 16, 16)], dst_ref=halo,
        send_sem=halo_sem.at[0], recv_sem=halo_sem.at[1],
        device_id={"ctx": lax.rem(me + 1, SHARDS)},
    )

    @pl.when(me < SHARDS - 1)
    def _():
        to_next.start()

    def stretch_state(c):
        to_end = jnp.exp2(inner[c, :, STRETCH - 1 :] - inner[c])
        parts = []
        for h in range(HEADS):
            x_h = jnp.concatenate(
                [xt[c, 0, h * HEAD_DIM : (h + 1) * HEAD_DIM], xt[c, 1, h * HEAD_DIM : (h + 1) * HEAD_DIM]],
                axis=1,
            )
            parts.append((x_h.astype(F32) * to_end[h : h + 1]).astype(BF16))
        state[c] = jnp.dot(
            jnp.concatenate(parts, axis=0), keys[c], preferred_element_type=F32
        )

    def late(i, _):
        stretch_state(PIECES - 1 - i)
        return 0

    lax.fori_loop(0, PIECES - 1, late, 0)

    @pl.when(me == 0)
    def _():
        halo[...] = jnp.zeros_like(halo)

    @pl.when(me > 0)
    def _():
        to_next.wait_recv()

    for group in range(6):
        chans = slice(group * HALF, (group + 1) * HALF)
        window = jnp.concatenate([halo[:, chans], x_ref[:HALF, chans]], axis=0).astype(F32)
        place(0, group, activate(window, conv_ref, chans))
    stretch_state(0)

    for h in range(HEADS):
        at = slice(h * HEAD_DIM, (h + 1) * HEAD_DIM)
        carried = state[0, at]
        for c in range(1, PIECES):
            low[c - 1, at] = carried.astype(BF16)
            fall = jnp.exp2(
                jnp.broadcast_to(inner[c, h : h + 1, STRETCH - 1 :], (1, STATE))
            )
            carried = fall * carried + state[c, at]
        send1[4 * h : 4 * (h + 1)] = carried.astype(BF16).reshape(4, ROWS, STATE)

    def spread(d, _):
        other = lax.rem(me + d, SHARDS)
        pltpu.make_async_remote_copy(
            src_ref=send1.at[other], dst_ref=recv1.at[me],
            send_sem=p1_send, recv_sem=p1_recv, device_id={"ctx": other},
        ).start()
        return 0

    lax.fori_loop(1, SHARDS, spread, 0)

    def spread_span(d, _):
        other = lax.rem(me + d, SHARDS)
        pltpu.make_async_remote_copy(
            src_ref=own_span, dst_ref=spans.at[me],
            send_sem=span_send, recv_sem=span_recv, device_id={"ctx": other},
        ).start()
        return 0

    lax.fori_loop(1, SHARDS, spread_span, 0)
    recv1[me] = send1[me]
    spans[me] = own_span[...]

    causal = (rows <= cols)[:HALF, :HALF]

    def near_own(c, before):
        q = [qt[c, 0], qt[c, 1]]
        k = keys[c]
        for half in range(2):
            width = HALF * (half + 1)
            score = jnp.dot(k[:width], q[half], preferred_element_type=F32)
            at_t = pl.ds(pl.multiple_of(c * STRETCH, STRETCH) + half * HALF, HALF)
            row_all = inner[c, :, half * HALF : (half + 1) * HALF]
            own_scale = level_ref[0, :, at_t]
            near_scale = level_ref[1, :, at_t] * jnp.exp2(row_all)
            if before:
                readout = jnp.dot(low[c - 1], q[half], preferred_element_type=F32)
            for h in range(HEADS):
                at = slice(h * HEAD_DIM, (h + 1) * HEAD_DIM)
                gap = row_all[h : h + 1] - column[c, :width, h : h + 1]
                blocks = []
                if half == 1:
                    blocks.append((jnp.exp2(gap[:HALF]) * score[:HALF]).astype(BF16))
                last = jnp.where(causal, gap[width - HALF :], -jnp.inf)
                blocks.append((jnp.exp2(last) * score[width - HALF :]).astype(BF16))
                own = jnp.dot(xt[c, half, at], blocks[-1], preferred_element_type=F32)
                if half == 1:
                    own = own + jnp.dot(xt[c, 0, at], blocks[0], preferred_element_type=F32)
                own = own * own_scale[h : h + 1]
                if before:
                    own = own + readout[at] * near_scale[h : h + 1]
                mixed[c, half, at] = own

    near_own(0, False)

    def rest(c, _):
        near_own(c, True)
        return 0

    lax.fori_loop(1, PIECES, rest, 0)

    pltpu.make_async_remote_copy(
        src_ref=send1.at[pl.ds(0, SHARDS - 1)], dst_ref=recv1.at[pl.ds(0, SHARDS - 1)],
        send_sem=p1_send, recv_sem=p1_recv, device_id={"ctx": lax.rem(me + 1, SHARDS)},
    ).wait()
    pltpu.make_async_remote_copy(
        src_ref=spans.at[pl.ds(0, SHARDS - 1)], dst_ref=spans.at[pl.ds(0, SHARDS - 1)],
        send_sem=span_send, recv_sem=span_recv, device_id={"ctx": lax.rem(me + 1, SHARDS)},
    ).wait()
    head = me // (SHARDS // HEADS)
    ends = [recv1[q].astype(F32) for q in range(SHARDS)]
    falls = [spans[q, pl.ds(head, 1)] for q in range(SHARDS)]
    for k in range(BITS):
        for group in range(0, len(ends), 2):
            left = ends[group].astype(BF16)
            for r in range((group + 1) << k, (group + 2) << k):
                stage[r * BITS + popcount(r % 2**k)] = left
        falls_next = [falls[i] + falls[i + 1] for i in range(0, len(falls), 2)]
        ends = [
            jnp.exp2(falls[i + 1]) * ends[i] + ends[i + 1] for i in range(0, len(ends), 2)
        ]
        falls = falls_next

    def answer(d, _):
        other = lax.rem(me + d, SHARDS)
        count = popcount(other)
        for n in range(1, BITS + 1):

            @pl.when(count == n)
            def _():
                pltpu.make_async_remote_copy(
                    src_ref=stage.at[pl.ds(other * BITS, n)],
                    dst_ref=recv3.at[pl.ds(me * BITS, n)],
                    send_sem=p3_send, recv_sem=p3_recv, device_id={"ctx": other},
                ).start()

        return 0

    lax.fori_loop(1, SHARDS, answer, 0)
    for n in range(1, BITS + 1):

        @pl.when(bits == n)
        def _():
            recv3[pl.ds(me * BITS, n)] = stage[pl.ds(me * BITS, n)]

    slot_weight[...] = jnp.zeros_like(slot_weight)
    for k in range(BITS):
        digit = (me // 2**k) % 2
        slot = popcount(me % 2**k)
        first = (me // 2**k) * 2**k

        @pl.when(digit == 1)
        def _():
            def add(q, total):
                return total + spans[q]

            between = lax.fori_loop(first, me, add, jnp.zeros((HEADS, HALF), F32))
            for c in range(PIECES):
                gap = between + jnp.zeros((HEADS, HALF), F32)
                for e in range(c):
                    gap = gap + jnp.broadcast_to(inner[e, :, STRETCH - 1 :], (HEADS, HALF))
                for half in range(2):
                    tokens = slice((2 * c + half) * HALF, (2 * c + half + 1) * HALF)
                    slot_weight[2 * c + half, slot] = level_ref[2 + k, :, tokens] * jnp.exp2(
                        gap + inner[c, :, half * HALF : (half + 1) * HALF]
                    )

    for n in range(1, BITS + 1):

        @pl.when(bits == n)
        def _():
            pltpu.make_async_remote_copy(
                src_ref=stage.at[pl.ds(0, (SHARDS - 1) * n)],
                dst_ref=recv3.at[pl.ds(0, (SHARDS - 1) * n)],
                send_sem=p3_send, recv_sem=p3_recv, device_id={"ctx": lax.rem(me + 1, SHARDS)},
            ).wait_recv()

    def finish(b, _):
        c, half = b // 2, b % 2
        q = qt[c, half]
        square = jnp.zeros((HEAD_DIM, HALF), F32)
        for h in range(HEADS):
            buckets = recv3[4 * BITS * h : 4 * BITS * (h + 1)].reshape(4 * BITS * ROWS, STATE)
            readout = jnp.dot(buckets, q, preferred_element_type=F32)
            weights = [slot_weight[b, j, h : h + 1] for j in range(BITS)]
            parts = []
            for piece in range(4):
                total = mixed[c, half, h * HEAD_DIM + piece * ROWS : h * HEAD_DIM + (piece + 1) * ROWS]
                for j in range(BITS):
                    at = (piece * BITS + j) * ROWS
                    total = total + readout[at : at + ROWS] * weights[j]
                parts.append(total)
            total = jnp.concatenate(parts, axis=0)
            mixed[c, half, h * HEAD_DIM : (h + 1) * HEAD_DIM] = total
            square = square + total * total
        mean = jnp.sum(square, axis=0, keepdims=True) * (1.0 / WIDTH)
        scale = lax.rsqrt(mean + 1e-05)
        for g in range(WIDTH // HALF):
            at = slice(g * HALF, (g + 1) * HALF)
            normed = (mixed[c, half, at] * scale * gain_col[at]).astype(BF16)
            out_ref[pl.ds(pl.multiple_of(b * HALF, HALF), HALF), at] = normed.T
        return 0

    lax.fori_loop(0, TOKENS // HALF, finish, 0)

    @pl.when(me < SHARDS - 1)
    def _():
        to_next.wait_send()

    for n in range(BITS + 1):

        @pl.when(bits == n)
        def _():
            pltpu.make_async_remote_copy(
                src_ref=stage.at[pl.ds(0, SHARDS * BITS // 2 - n)],
                dst_ref=recv3.at[pl.ds(0, SHARDS * BITS // 2 - n)],
                send_sem=p3_send, recv_sem=p3_recv, device_id={"ctx": lax.rem(me + 1, SHARDS)},
            ).wait_send()


def per_device(mixer_input, conv_weight, log_decay, level_weight, norm_gain):
    vmem = pl.BlockSpec(memory_space=pltpu.VMEM)
    return pl.pallas_call(
        kernel,
        out_shape=jax.ShapeDtypeStruct((TOKENS, WIDTH), BF16),
        in_specs=[vmem] * 5,
        out_specs=vmem,
        scratch_shapes=[
            pltpu.VMEM((16, WIDTH + 2 * STATE), BF16),
            pltpu.VMEM((PIECES, 2, WIDTH, HALF), BF16),
            pltpu.VMEM((PIECES, STRETCH, STATE), BF16),
            pltpu.VMEM((PIECES, 2, STATE, HALF), BF16),
            pltpu.VMEM((PIECES, HEADS, STRETCH), F32),
            pltpu.VMEM((PIECES, STRETCH, HEADS), F32),
            pltpu.VMEM((PIECES, WIDTH, STATE), F32),
            pltpu.VMEM((PIECES - 1, WIDTH, STATE), BF16),
            pltpu.VMEM((PIECES, 2, WIDTH, HALF), F32),
            pltpu.VMEM((WIDTH, 1), F32),
            pltpu.VMEM((TOKENS // HALF, BITS, HEADS, HALF), F32),
            pltpu.VMEM((SHARDS, ROWS, STATE), BF16),
            pltpu.VMEM((SHARDS, ROWS, STATE), BF16),
            pltpu.VMEM((HEADS, HALF), F32),
            pltpu.VMEM((SHARDS, HEADS, HALF), F32),
            pltpu.VMEM((SHARDS * BITS, ROWS, STATE), BF16),
            pltpu.VMEM((SHARDS * BITS, ROWS, STATE), BF16),
            pltpu.SemaphoreType.DMA((2,)),
            pltpu.SemaphoreType.DMA,
            pltpu.SemaphoreType.DMA,
            pltpu.SemaphoreType.DMA,
            pltpu.SemaphoreType.DMA,
            pltpu.SemaphoreType.DMA,
            pltpu.SemaphoreType.DMA,
        ],
        compiler_params=pltpu.CompilerParams(
            collective_id=0, has_side_effects=True, vmem_limit_bytes=40 << 20
        ),
    )(mixer_input, conv_weight, log_decay, level_weight, norm_gain.reshape(1, WIDTH))


def solution(mesh):
    placed = (
        P("ctx", "heads"),
        P(None, "heads"),
        P("heads", "ctx"),
        P(None, "heads", "ctx"),
        P("heads"),
    )
    return jax.shard_map(
        per_device, mesh=mesh, in_specs=placed, out_specs=P("ctx", "heads"), check_vma=False
    )
```

time: 175 us -> 41.7 us (0.24)
  the two profiles are of different devices: /device:TPU:2 before, /device:TPU:8 now
where the time goes in v1:
time: 41.7 us; the launch traced here: 41.5 us
  Pallas kernels  36 us (86%)
  local copies, waits for them, and re-layouts  5.46 us (13%)
    pallas_call x1, Pallas kernels, per_device(): pl.pallas_call(kernel, out_shape=jax.ShapeDtypeStruct((TOKENS, WIDTH), BF...  36 us
    unnamed x11, local copies, waits for them, and re-layouts  5.46 us

profile of v1, /device:TPU:8, one launch (start us, length us, event | category | flops | bytes accessed | tf_op | source)
XLA Modules:
  0.0 41.5 jit_solution(10094571759299540378)
XLA Ops:
  0.0 0.0 copy-start
  0.0 1.4 %copy-done = bf16[1024,768]{1,0:T(8,128)(2,1)S(1)} copy-done((bf16[1024,768]{1,0:T(8,128)(2,1)S(1)}, bf16[1024,768]{1,0:T(8,128)(2,1)}, u32[]{:S(2)}) %copy-start) | copy-done | bytes 1572888
  1.4 0.0 copy-start.1
  1.4 0.9 %copy-done.1 = f32[7,8,1024]{2,1,0:T(8,128)S(1)} copy-done((f32[7,8,1024]{2,1,0:T(8,128)S(1)}, f32[7,8,1024]{2,1,0:T(8,128)}, u32[]{:S(2)}) %copy-start.1) | copy-done | bytes 229400
  2.3 0.0 copy-start.2
  2.4 0.8 %copy-done.2 = f32[8,1024]{1,0:T(8,128)S(1)} copy-done((f32[8,1024]{1,0:T(8,128)S(1)}, f32[8,1024]{1,0:T(8,128)}, u32[]{:S(2)}) %copy-start.2) | copy-done | bytes 32792
  3.1 0.0 copy-start.3
  3.1 0.7 %copy-done.3 = f32[4,768]{1,0:T(4,128)S(1)} copy-done((f32[4,768]{1,0:T(4,128)S(1)}, f32[4,768]{1,0:T(4,128)}, u32[]{:S(2)}) %copy-start.3) | copy-done | bytes 12312
  3.8 0.0 copy-start.4
  3.8 0.7 %copy-done.4 = f32[512]{0:T(512)S(1)} copy-done((f32[512]{0:T(512)S(1)}, f32[512]{0:T(512)}, u32[]{:S(2)}) %copy-start.4) | copy-done | bytes 2072
  4.5 36.0 %shard_map.55 = bf16[1024,512]{1,0:T(8,128)(2,1)S(1)} custom-call(bf16[1024,768]{1,0:T(8,128)(2,1)S(1)} %copy-done, f32[4,768]{1,0:T(4,128)S(1)} %copy-done.3, f32[8,1024]{1,0:T(8,128)S(1)} %copy-done.2, f32[7,8,1024]{2,1,0:T(8,128)S(1)} %copy-done.1, f32[1,512]{1,0:T(1,128)S(1)} %bitcast.1), custom_call_target="tpu_custom_call" | custom-call | tf_op jit(solution)/shard_map/pallas_call | solution.py:340
  40.5 1.0 %copy.7 = bf16[1024,512]{1,0:T(8,128)(2,1)} copy(bf16[1024,512]{1,0:T(8,128)(2,1)S(1)} %shard_map.55) | data formatting | bytes 2097152
Async XLA Ops:
  0.0 1.4 %copy-start = (bf16[1024,768]{1,0:T(8,128)(2,1)S(1)}, bf16[1024,768]{1,0:T(8,128)(2,1)}, u32[]{:S(2)}) copy-start(bf16[1024,768]{1,0:T(8,128)(2,1)} %x_ref.1) | copy-start | bytes 4718596
  1.4 0.9 %copy-start.1 = (f32[7,8,1024]{2,1,0:T(8,128)S(1)}, f32[7,8,1024]{2,1,0:T(8,128)}, u32[]{:S(2)}) copy-start(f32[7,8,1024]{2,1,0:T(8,128)} %level_ref.1) | copy-start | bytes 688132
  2.3 0.8 %copy-start.2 = (f32[8,1024]{1,0:T(8,128)S(1)}, f32[8,1024]{1,0:T(8,128)}, u32[]{:S(2)}) copy-start(f32[8,1024]{1,0:T(8,128)} %rate_ref.1) | copy-start | bytes 98308
  3.1 0.7 %copy-start.3 = (f32[4,768]{1,0:T(4,128)S(1)}, f32[4,768]{1,0:T(4,128)}, u32[]{:S(2)}) copy-start(f32[4,768]{1,0:T(4,128)} %conv_ref.1) | copy-start | bytes 36868
  3.8 0.7 %copy-start.4 = (f32[512]{0:T(512)S(1)}, f32[512]{0:T(512)}, u32[]{:S(2)}) copy-start(f32[512]{0:T(512)} %param.9) | copy-start | bytes 6148

commit v2 on v1

v2 whole, which is shorter than its diff:
```python
import functools

import jax
import jax.numpy as jnp
from jax import lax
from jax.experimental import pallas as pl
from jax.experimental.pallas import tpu as pltpu
from jax.sharding import PartitionSpec as P

HEADS = 8
HEAD_DIM = 64
STATE = 128
STRETCH = 256
WIDTH = 512
TOKENS = 1024
PIECES = TOKENS // STRETCH
SHARDS = 32
ALONG_Z = 8
ALONG_Y = 4
BITS = 5
HALF = 128
GROUP = 16
ROWS = WIDTH // GROUP
MIDDLE = 3
LOG2E = 1.4426950408889634

NT = (((1,), (1,)), ((), ()))
F32 = jnp.float32
BF16 = jnp.bfloat16


def popcount(r):
    count = r % 2
    for k in range(1, BITS):
        count = count + (r // 2**k) % 2
    return count


def activate(window, conv_ref, cols):
    total = conv_ref[3:4, cols] * window[16:144]
    for j in range(3):
        total = total + conv_ref[j : j + 1, cols] * window[13 + j : 141 + j]
    half = 0.5 * total
    return (half + half * jnp.tanh(half)).astype(BF16)


def kernel(
    x_hbm, conv_hbm, rate_hbm, level_hbm, gain_hbm, out_ref,
    x_ref, conv_ref, rate_ref, level_ref, gain_ref, halo, xt, keys, qt, inner, column, state, low, mixed, gain_col, slot_weight,
    send1, recv1, spans, stage, top, recv3,
    in_sem, x_sem, halo_sem, p1_send, p1_recv, span_sem, p0_sem, p4_sem, p3_send, p3_recv,
):
    me = lax.axis_index("ctx")
    bits = popcount(me)
    pair = me // GROUP
    place_in = lax.rem(me, GROUP)
    odd = lax.rem(me, 2)
    middle = popcount(place_in // 2)

    barrier = pltpu.get_barrier_semaphore()

    small_in = [
        pltpu.make_async_copy(src, dst, in_sem.at[i])
        for i, (src, dst) in enumerate(
            ((rate_hbm, rate_ref), (conv_hbm, conv_ref), (gain_hbm, gain_ref), (level_hbm, level_ref))
        )
    ]

    def rows_in(start, count, at):
        span_of = pl.ds(start, count)
        return pltpu.make_async_copy(x_hbm.at[span_of], x_ref.at[span_of], x_sem.at[at])

    def stretch_in(c):
        return rows_in(pl.multiple_of(c * STRETCH - 16, 16), STRETCH, c)

    head_in = rows_in(0, STRETCH - 16, 0)
    tail_in = rows_in(TOKENS - 16, 16, PIECES)
    for copy in small_in[:3]:
        copy.start()
    tail_in.start()
    for c in range(PIECES - 1, 0, -1):
        stretch_in(c).start()
    head_in.start()
    small_in[3].start()

    def greet(d, _):
        other = lax.rem(me + d, SHARDS)
        pl.semaphore_signal(barrier, inc=1, device_id={"ctx": other})
        return 0

    lax.fori_loop(1, SHARDS, greet, 0)

    small_in[0].wait()
    rows = lax.broadcasted_iota(jnp.int32, (STRETCH, STRETCH), 0)
    cols = lax.broadcasted_iota(jnp.int32, (STRETCH, STRETCH), 1)
    lower = jnp.where(rows >= cols, 1.0, 0.0).astype(F32)
    span = jnp.zeros((HEADS, HALF), F32)
    for c in range(PIECES):
        rate = rate_ref[:, c * STRETCH : (c + 1) * STRETCH] * LOG2E
        inner[c] = lax.dot_general(
            rate, lower, NT, precision=lax.Precision.HIGHEST, preferred_element_type=F32
        )
        column[c] = lax.dot_general(
            lower, rate, NT, precision=lax.Precision.HIGHEST, preferred_element_type=F32
        )
        span = span + jnp.broadcast_to(inner[c, :, STRETCH - 1 :], (HEADS, HALF))
    spans[me] = span

    small_in[1].wait()
    small_in[2].wait()
    diag = (rows == cols)[:HALF, :HALF]
    for g in range(WIDTH // HALF):
        row = jnp.broadcast_to(gain_ref[:, g * HALF : (g + 1) * HALF], (HALF, HALF))
        gain_col[g * HALF : (g + 1) * HALF] = jnp.sum(
            jnp.where(diag, row, 0.0), axis=1, keepdims=True
        )

    row_start = me - lax.rem(me, ALONG_Z)

    def to_row(d):
        return row_start + lax.rem(me + d, ALONG_Z)

    def to_column(d):
        return lax.rem(me + d * ALONG_Z, SHARDS)

    def span_along_row(d):
        return pltpu.make_async_remote_copy(
            src_ref=spans.at[me], dst_ref=spans.at[me],
            send_sem=span_sem.at[0], recv_sem=span_sem.at[1], device_id={"ctx": to_row(d)},
        )

    def span_along_column(d):
        at = pl.ds(row_start, ALONG_Z)
        return pltpu.make_async_remote_copy(
            src_ref=spans.at[at], dst_ref=spans.at[at],
            send_sem=span_sem.at[2], recv_sem=span_sem.at[3], device_id={"ctx": to_column(d)},
        )

    def wait_bytes(ref, count, send_sem, recv_sem):
        part = ref.at[pl.ds(0, count)]
        return pltpu.make_async_remote_copy(
            src_ref=part, dst_ref=part, send_sem=send_sem, recv_sem=recv_sem,
            device_id={"ctx": lax.rem(me + 1, SHARDS)},
        )

    to_next = pltpu.make_async_remote_copy(
        src_ref=x_hbm.at[pl.ds(TOKENS - 16, 16)], dst_ref=halo,
        send_sem=halo_sem.at[0], recv_sem=halo_sem.at[1],
        device_id={"ctx": lax.rem(me + 1, SHARDS)},
    )

    def place(b, group, act):
        c, half = b // 2, b % 2
        if group < 4:
            xt[c, half, group * HALF : (group + 1) * HALF] = act.T
        elif group == 4:
            keys[c, pl.ds(pl.multiple_of(half * HALF, HALF), HALF)] = act
        else:
            qt[c, half] = act.T

    def block(b):
        start = pl.multiple_of(b * HALF - 16, 16)
        for group in range(6):
            chans = slice(group * HALF, (group + 1) * HALF)
            window = x_ref[pl.ds(start, HALF + 16), chans].astype(F32)
            place(b, group, activate(window, conv_ref, chans))

    def stretch_state(c):
        to_end = jnp.exp2(inner[c, :, STRETCH - 1 :] - inner[c])
        parts = []
        for h in range(HEADS):
            x_h = jnp.concatenate(
                [xt[c, 0, h * HEAD_DIM : (h + 1) * HEAD_DIM], xt[c, 1, h * HEAD_DIM : (h + 1) * HEAD_DIM]],
                axis=1,
            )
            parts.append((x_h.astype(F32) * to_end[h : h + 1]).astype(BF16))
        state[c] = jnp.dot(
            jnp.concatenate(parts, axis=0), keys[c], preferred_element_type=F32
        )

    tail_in.wait()

    def late(i, _):
        c = PIECES - 1 - i
        stretch_in(c).wait()
        lax.fori_loop(0, 2, lambda half, _: (block(2 * c + 1 - half), 0)[1], 0)
        stretch_state(c)

        @pl.when(i == 0)
        def _():
            pl.semaphore_wait(barrier, SHARDS - 1)

            @pl.when(me < SHARDS - 1)
            def _():
                to_next.start()

            for d in range(1, ALONG_Z):
                span_along_row(d).start()

        return 0

    lax.fori_loop(0, PIECES - 1, late, 0)
    head_in.wait()
    block(1)

    @pl.when(me == 0)
    def _():
        halo[...] = jnp.zeros_like(halo)

    @pl.when(me > 0)
    def _():
        to_next.wait_recv()


    for group in range(6):
        chans = slice(group * HALF, (group + 1) * HALF)
        window = jnp.concatenate([halo[:, chans], x_ref[:HALF, chans]], axis=0).astype(F32)
        place(0, group, activate(window, conv_ref, chans))
    stretch_state(0)

    for h in range(HEADS):
        at = slice(h * HEAD_DIM, (h + 1) * HEAD_DIM)
        carried = state[0, at]
        for c in range(1, PIECES):
            low[c - 1, at] = carried.astype(BF16)
            fall = jnp.exp2(
                jnp.broadcast_to(inner[c, h : h + 1, STRETCH - 1 :], (1, STATE))
            )
            carried = fall * carried + state[c, at]
        send1[2 * h : 2 * (h + 1)] = carried.astype(BF16).reshape(2, ROWS, STATE)

    def spread(d, _):
        there = lax.rem(place_in + d, GROUP)
        pltpu.make_async_remote_copy(
            src_ref=send1.at[there], dst_ref=recv1.at[place_in],
            send_sem=p1_send, recv_sem=p1_recv, device_id={"ctx": pair * GROUP + there},
        ).start()
        return 0

    lax.fori_loop(1, GROUP, spread, 0)
    recv1[place_in] = send1[place_in]

    causal = (rows <= cols)[:HALF, :HALF]

    def near_own(c, before):
        q = [qt[c, 0], qt[c, 1]]
        k = keys[c]
        for half in range(2):
            width = HALF * (half + 1)
            score = jnp.dot(k[:width], q[half], preferred_element_type=F32)
            at_t = pl.ds(pl.multiple_of(c * STRETCH, STRETCH) + half * HALF, HALF)
            row_all = inner[c, :, half * HALF : (half + 1) * HALF]
            own_scale = level_ref[0, :, at_t]
            near_scale = level_ref[1, :, at_t] * jnp.exp2(row_all)
            if before:
                readout = jnp.dot(low[c - 1], q[half], preferred_element_type=F32)
            for h in range(HEADS):
                at = slice(h * HEAD_DIM, (h + 1) * HEAD_DIM)
                gap = row_all[h : h + 1] - column[c, :width, h : h + 1]
                blocks = []
                if half == 1:
                    blocks.append((jnp.exp2(gap[:HALF]) * score[:HALF]).astype(BF16))
                last = jnp.where(causal, gap[width - HALF :], -jnp.inf)
                blocks.append((jnp.exp2(last) * score[width - HALF :]).astype(BF16))
                own = jnp.dot(xt[c, half, at], blocks[-1], preferred_element_type=F32)
                if half == 1:
                    own = own + jnp.dot(xt[c, 0, at], blocks[0], preferred_element_type=F32)
                own = own * own_scale[h : h + 1]
                if before:
                    own = own + readout[at] * near_scale[h : h + 1]
                mixed[c, half, at] = own

    small_in[3].wait()
    near_own(0, False)
    wait_bytes(spans, ALONG_Z - 1, span_sem.at[0], span_sem.at[1]).wait()
    for d in range(1, ALONG_Y):
        span_along_column(d).start()

    neighbour = pltpu.make_async_remote_copy(
        src_ref=send1, dst_ref=recv3.at[pair],
        send_sem=p0_sem.at[0], recv_sem=p0_sem.at[1],
        device_id={"ctx": lax.rem(me + 1, SHARDS)},
    )

    def rest(c, _):
        near_own(c, True)

        @pl.when((odd == 0) & (c == 1))
        def _():
            neighbour.start()

        return 0

    lax.fori_loop(1, PIECES, rest, 0)

    wait_bytes(recv1, GROUP - 1, p1_send, p1_recv).wait()
    wait_bytes(spans, SHARDS - ALONG_Z, span_sem.at[2], span_sem.at[3]).wait()
    head = place_in // (GROUP // HEADS)
    ends = [recv1[q].astype(F32) for q in range(GROUP)]
    falls = [spans[pair * GROUP + q, pl.ds(head, 1)] for q in range(GROUP)]
    for k in range(BITS - 1):
        if k > 0:
            for group in range(0, len(ends), 2):
                left = ends[group].astype(BF16)
                for r in range((group + 1) << k, (group + 2) << k):
                    stage[popcount((r // 2) % 2 ** (k - 1)), r] = left
        ends = [
            jnp.exp2(falls[i + 1]) * ends[i] + ends[i + 1] for i in range(0, len(ends), 2)
        ]
        falls = [falls[i] + falls[i + 1] for i in range(0, len(falls), 2)]
    top[...] = ends[0].astype(BF16)

    def answer(i, _):
        early = jnp.where(i < 4, 1, 0)
        turn = lax.rem(place_in + i, 4) * early + lax.rem(place_in + i, 12) * (1 - early)
        there = early * ((turn // 2) * ALONG_Z + turn % 2) + (1 - early) * ((turn // 6) * ALONG_Z + 2 + turn % 6)
        @pl.when(pair == 0)
        def _():
            pltpu.make_async_remote_copy(
                src_ref=top, dst_ref=recv3.at[0, place_in],
                send_sem=p4_sem.at[0], recv_sem=p4_sem.at[1],
                device_id={"ctx": GROUP + there},
            ).start()

        count = popcount(there // 2) * jnp.where(there == place_in, 0, 1)
        for n in range(1, MIDDLE + 1):

            @pl.when(count == n)
            def _():
                pltpu.make_async_remote_copy(
                    src_ref=stage.at[pl.ds(0, n), there],
                    dst_ref=recv3.at[pl.ds(pair + lax.rem(there, 2), n), place_in],
                    send_sem=p3_send, recv_sem=p3_recv,
                    device_id={"ctx": pair * GROUP + there},
                ).start()

        return 0

    lax.fori_loop(0, GROUP, answer, 0)
    for n in range(1, MIDDLE + 1):

        @pl.when(middle == n)
        def _():
            recv3[pl.ds(pair + odd, n), place_in] = stage[:n, place_in]

    for k in range(BITS):
        digit = (me // 2**k) % 2
        if k == 0:
            slot = pair
        elif k == BITS - 1:
            slot = 0
        else:
            slot = pair + odd + popcount((me // 2) % 2 ** (k - 1))
        first = (me // 2**k) * 2**k

        @pl.when(digit == 1)
        def _():
            def add(q, total):
                return total + spans[q]

            between = lax.fori_loop(first, me, add, jnp.zeros((HEADS, HALF), F32))
            for c in range(PIECES):
                gap = between + jnp.zeros((HEADS, HALF), F32)
                for e in range(c):
                    gap = gap + jnp.broadcast_to(inner[e, :, STRETCH - 1 :], (HEADS, HALF))
                for half in range(2):
                    tokens = slice((2 * c + half) * HALF, (2 * c + half + 1) * HALF)
                    slot_weight[2 * c + half, slot] = level_ref[2 + k, :, tokens] * jnp.exp2(
                        gap + inner[c, :, half * HALF : (half + 1) * HALF]
                    )

    @pl.when(odd == 1)
    def _():
        neighbour.wait_recv()

    for n in range(1, MIDDLE + 1):

        @pl.when(middle == n)
        def _():
            part = recv3.at[pl.ds(0, n), pl.ds(0, GROUP - 1)]
            pltpu.make_async_remote_copy(
                src_ref=part, dst_ref=part, send_sem=p3_send, recv_sem=p3_recv,
                device_id={"ctx": lax.rem(me + 1, SHARDS)},
            ).wait_recv()

    @pl.when(pair == 1)
    def _():
        wait_bytes(recv1, GROUP, p4_sem.at[0], p4_sem.at[1]).wait_recv()

    def finish(c, _):
        q = jnp.concatenate([qt[c, 0], qt[c, 1]], axis=1)

        def add_bucket(j, _):
            for g in range(4):
                bucket = recv3[j, g * 4 : (g + 1) * 4].reshape(HALF, STATE)
                readout = jnp.dot(bucket, q, preferred_element_type=F32)
                for half in range(2):
                    lanes = slice(half * HALF, (half + 1) * HALF)
                    for h in range(2):
                        at = slice(h * HEAD_DIM, (h + 1) * HEAD_DIM)
                        to = slice(g * HALF + h * HEAD_DIM, g * HALF + (h + 1) * HEAD_DIM)
                        weight = slot_weight[2 * c + half, j, 2 * g + h : 2 * g + h + 1]
                        mixed[c, half, to] = mixed[c, half, to] + readout[at, lanes] * weight
            return 0

        lax.fori_loop(0, bits, add_bucket, 0)
        for half in range(2):
            square = jnp.zeros((HEAD_DIM, HALF), F32)
            for h in range(HEADS):
                part = mixed[c, half, h * HEAD_DIM : (h + 1) * HEAD_DIM]
                square = square + part * part
            mean = jnp.sum(square, axis=0, keepdims=True) * (1.0 / WIDTH)
            scale = lax.rsqrt(mean + 1e-05)
            for g in range(WIDTH // HALF):
                at = slice(g * HALF, (g + 1) * HALF)
                normed = (mixed[c, half, at] * scale * gain_col[at]).astype(BF16)
                tokens = pl.ds(pl.multiple_of(c * STRETCH, STRETCH) + half * HALF, HALF)
                out_ref[tokens, at] = normed.T
        return 0

    lax.fori_loop(0, PIECES, finish, 0)

    @pl.when(me < SHARDS - 1)
    def _():
        to_next.wait_send()

    @pl.when(odd == 0)
    def _():
        neighbour.wait_send()

    @pl.when(pair == 0)
    def _():
        wait_bytes(recv1, GROUP, p4_sem.at[0], p4_sem.at[1]).wait_send()

    for n in range(MIDDLE + 1):

        @pl.when(middle == n)
        def _():
            for part in (stage.at[0], stage.at[1, pl.ds(0, GROUP // 2 - n)]):
                pltpu.make_async_remote_copy(
                    src_ref=part, dst_ref=part, send_sem=p3_send, recv_sem=p3_recv,
                    device_id={"ctx": lax.rem(me + 1, SHARDS)},
                ).wait_send()


def per_device(mixer_input, conv_weight, log_decay, level_weight, norm_gain):
    vmem = pl.BlockSpec(memory_space=pltpu.VMEM)
    hbm = pl.BlockSpec(memory_space=pltpu.HBM)
    return pl.pallas_call(
        kernel,
        out_shape=jax.ShapeDtypeStruct((TOKENS, WIDTH), BF16),
        in_specs=[hbm] * 5,
        out_specs=vmem,
        scratch_shapes=[
            pltpu.VMEM((TOKENS, WIDTH + 2 * STATE), BF16),
            pltpu.VMEM((4, WIDTH + 2 * STATE), F32),
            pltpu.VMEM((HEADS, TOKENS), F32),
            pltpu.VMEM((2 + BITS, HEADS, TOKENS), F32),
            pltpu.VMEM((1, WIDTH), F32),
            pltpu.VMEM((16, WIDTH + 2 * STATE), BF16),
            pltpu.VMEM((PIECES, 2, WIDTH, HALF), BF16),
            pltpu.VMEM((PIECES, STRETCH, STATE), BF16),
            pltpu.VMEM((PIECES, 2, STATE, HALF), BF16),
            pltpu.VMEM((PIECES, HEADS, STRETCH), F32),
            pltpu.VMEM((PIECES, STRETCH, HEADS), F32),
            pltpu.VMEM((PIECES, WIDTH, STATE), F32),
            pltpu.VMEM((PIECES - 1, WIDTH, STATE), BF16),
            pltpu.VMEM((PIECES, 2, WIDTH, HALF), F32),
            pltpu.VMEM((WIDTH, 1), F32),
            pltpu.VMEM((TOKENS // HALF, BITS, HEADS, HALF), F32),
            pltpu.VMEM((GROUP, ROWS, STATE), BF16),
            pltpu.VMEM((GROUP, ROWS, STATE), BF16),
            pltpu.VMEM((SHARDS, HEADS, HALF), F32),
            pltpu.VMEM((MIDDLE, GROUP, ROWS, STATE), BF16),
            pltpu.VMEM((ROWS, STATE), BF16),
            pltpu.VMEM((BITS, GROUP, ROWS, STATE), BF16),
            pltpu.SemaphoreType.DMA((4,)),
            pltpu.SemaphoreType.DMA((PIECES + 1,)),
            pltpu.SemaphoreType.DMA((2,)),
            pltpu.SemaphoreType.DMA,
            pltpu.SemaphoreType.DMA,
            pltpu.SemaphoreType.DMA((4,)),
            pltpu.SemaphoreType.DMA((2,)),
            pltpu.SemaphoreType.DMA((2,)),
            pltpu.SemaphoreType.DMA,
            pltpu.SemaphoreType.DMA,
        ],
        compiler_params=pltpu.CompilerParams(
            collective_id=0, has_side_effects=True, vmem_limit_bytes=63 << 20
        ),
    )(mixer_input, conv_weight, log_decay, level_weight, norm_gain.reshape(1, WIDTH))


def solution(mesh):
    placed = (
        P("ctx", "heads"),
        P(None, "heads"),
        P("heads", "ctx"),
        P(None, "heads", "ctx"),
        P("heads"),
    )
    return jax.shard_map(
        per_device, mesh=mesh, in_specs=placed, out_specs=P("ctx", "heads"), check_vma=False
    )
```

time: 41.7 us -> 35.2 us (0.84)
  the two profiles are of different devices: /device:TPU:8 before, /device:TPU:252 now
where the time goes in v2:
time: 35.2 us; the launch traced here: 35.1 us
  Pallas kernels  32.8 us (93%)
  local copies, waits for them, and re-layouts  2.26 us (6%)
    pallas_call x1, Pallas kernels, per_device(): pl.pallas_call(kernel, out_shape=jax.ShapeDtypeStruct((TOKENS, WIDTH), BF...  32.8 us
    unnamed x1, local copies, waits for them, and re-layouts  2.26 us

profile of v2, /device:TPU:252, one launch (start us, length us, event | category | flops | bytes accessed | tf_op | source)
XLA Modules:
  0.0 35.1 jit_solution(17021357252661780015)
XLA Ops:
  0.0 32.8 %shard_map.55 = bf16[1024,512]{1,0:T(8,128)(2,1)} custom-call(bf16[1024,768]{1,0:T(8,128)(2,1)} %x_hbm.1, f32[4,768]{1,0:T(4,128)} %conv_hbm.1, f32[8,1024]{1,0:T(8,128)} %rate_hbm.1, f32[7,8,1024]{2,1,0:T(8,128)} %level_hbm.1, f32[1,512]{1,0:T(1,128)} %bitcast.1), custom_call_target="tpu_custom_call" | custom-call | tf_op jit(solution)/shard_map/pallas_call | solution.py:449
  32.8 2.3 %copy.7 = bf16[1024,512]{1,0:T(8,128)(2,1)} copy(bf16[1024,512]{1,0:T(8,128)(2,1)} %shard_map.55) | data formatting | bytes 2097152

commit v3 on v2

--- a/solution.py
+++ b/solution.py
@@ -45,10 +45,10 @@
 
 
 def kernel(
-    x_hbm, conv_hbm, rate_hbm, level_hbm, gain_hbm, out_ref,
-    x_ref, conv_ref, rate_ref, level_ref, gain_ref, halo, xt, keys, qt, inner, column, state, low, mixed, gain_col, slot_weight,
+    x_hbm, conv_hbm, rate_hbm, level_hbm, gain_hbm, out_hbm,
+    out_ref, x_ref, conv_ref, rate_ref, level_ref, gain_ref, halo, xt, keys, qt, inner, column, state, low, mixed, gain_col, slot_weight,
     send1, recv1, spans, stage, top, recv3,
-    in_sem, x_sem, halo_sem, p1_send, p1_recv, span_sem, p0_sem, p4_sem, p3_send, p3_recv,
+    in_sem, x_sem, out_sem, halo_sem, p1_send, p1_recv, span_sem, p0_sem, p4_sem, p3_send, p3_recv,
 ):
     me = lax.axis_index("ctx")
     bits = popcount(me)
@@ -94,26 +94,19 @@
     rows = lax.broadcasted_iota(jnp.int32, (STRETCH, STRETCH), 0)
     cols = lax.broadcasted_iota(jnp.int32, (STRETCH, STRETCH), 1)
     lower = jnp.where(rows >= cols, 1.0, 0.0).astype(F32)
+    rates = jnp.concatenate(
+        [rate_ref[:, c * STRETCH : (c + 1) * STRETCH] for c in range(PIECES)], axis=0
+    )
+    sums = lax.dot_general(
+        rates * LOG2E, lower, NT, precision=lax.Precision.HIGHEST, preferred_element_type=F32
+    )
     span = jnp.zeros((HEADS, HALF), F32)
     for c in range(PIECES):
-        rate = rate_ref[:, c * STRETCH : (c + 1) * STRETCH] * LOG2E
-        inner[c] = lax.dot_general(
-            rate, lower, NT, precision=lax.Precision.HIGHEST, preferred_element_type=F32
-        )
-        column[c] = lax.dot_general(
-            lower, rate, NT, precision=lax.Precision.HIGHEST, preferred_element_type=F32
-        )
-        span = span + jnp.broadcast_to(inner[c, :, STRETCH - 1 :], (HEADS, HALF))
+        part = sums[c * HEADS : (c + 1) * HEADS]
+        inner[c] = part
+        span = span + jnp.broadcast_to(part[:, STRETCH - 1 :], (HEADS, HALF))
     spans[me] = span
-
     small_in[1].wait()
-    small_in[2].wait()
-    diag = (rows == cols)[:HALF, :HALF]
-    for g in range(WIDTH // HALF):
-        row = jnp.broadcast_to(gain_ref[:, g * HALF : (g + 1) * HALF], (HALF, HALF))
-        gain_col[g * HALF : (g + 1) * HALF] = jnp.sum(
-            jnp.where(diag, row, 0.0), axis=1, keepdims=True
-        )
 
     row_start = me - lax.rem(me, ALONG_Z)
 
@@ -240,6 +233,18 @@
     lax.fori_loop(1, GROUP, spread, 0)
     recv1[place_in] = send1[place_in]
 
+    small_in[2].wait()
+    diag = (rows == cols)[:HALF, :HALF]
+    for g in range(WIDTH // HALF):
+        row = jnp.broadcast_to(gain_ref[:, g * HALF : (g + 1) * HALF], (HALF, HALF))
+        gain_col[g * HALF : (g + 1) * HALF] = jnp.sum(
+            jnp.where(diag, row, 0.0), axis=1, keepdims=True
+        )
+    for c in range(PIECES):
+        rate = rate_ref[:, c * STRETCH : (c + 1) * STRETCH] * LOG2E
+        column[c] = lax.dot_general(
+            lower, rate, NT, precision=lax.Precision.HIGHEST, preferred_element_type=F32
+        )
     causal = (rows <= cols)[:HALF, :HALF]
 
     def near_own(c, before):
@@ -369,56 +374,56 @@
                         gap + inner[c, :, half * HALF : (half + 1) * HALF]
                     )
 
-    @pl.when(odd == 1)
-    def _():
-        neighbour.wait_recv()
-
-    for n in range(1, MIDDLE + 1):
-
-        @pl.when(middle == n)
-        def _():
-            part = recv3.at[pl.ds(0, n), pl.ds(0, GROUP - 1)]
-            pltpu.make_async_remote_copy(
-                src_ref=part, dst_ref=part, send_sem=p3_send, recv_sem=p3_recv,
-                device_id={"ctx": lax.rem(me + 1, SHARDS)},
-            ).wait_recv()
-
-    @pl.when(pair == 1)
-    def _():
-        wait_bytes(recv1, GROUP, p4_sem.at[0], p4_sem.at[1]).wait_recv()
-
-    def finish(c, _):
-        q = jnp.concatenate([qt[c, 0], qt[c, 1]], axis=1)
-
-        def add_bucket(j, _):
+    def add_bucket(i, _):
+        slot = lax.rem(pair + i, bits)
+
+        @pl.when((odd == 1) & (i == 0))
+        def _():
+            neighbour.wait_recv()
+
+        for n in range(1, MIDDLE + 1):
+
+            @pl.when((middle == n) & (i == odd))
+            def _():
+                part = recv3.at[pl.ds(0, n), pl.ds(0, GROUP - 1)]
+                pltpu.make_async_remote_copy(
+                    src_ref=part, dst_ref=part, send_sem=p3_send, recv_sem=p3_recv,
+                    device_id={"ctx": lax.rem(me + 1, SHARDS)},
+                ).wait_recv()
+
+        @pl.when((pair == 1) & (i == bits - 1))
+        def _():
+            wait_bytes(recv1, GROUP, p4_sem.at[0], p4_sem.at[1]).wait_recv()
+
+        for c in range(PIECES):
+            q = jnp.concatenate([qt[c, 0], qt[c, 1]], axis=1)
             for g in range(4):
-                bucket = recv3[j, g * 4 : (g + 1) * 4].reshape(HALF, STATE)
+                bucket = recv3[slot, g * 4 : (g + 1) * 4].reshape(HALF, STATE)
                 readout = jnp.dot(bucket, q, preferred_element_type=F32)
                 for half in range(2):
                     lanes = slice(half * HALF, (half + 1) * HALF)
                     for h in range(2):
                         at = slice(h * HEAD_DIM, (h + 1) * HEAD_DIM)
                         to = slice(g * HALF + h * HEAD_DIM, g * HALF + (h + 1) * HEAD_DIM)
-                        weight = slot_weight[2 * c + half, j, 2 * g + h : 2 * g + h + 1]
+                        weight = slot_weight[2 * c + half, slot, 2 * g + h : 2 * g + h + 1]
                         mixed[c, half, to] = mixed[c, half, to] + readout[at, lanes] * weight
-            return 0
-
-        lax.fori_loop(0, bits, add_bucket, 0)
-        for half in range(2):
-            square = jnp.zeros((HEAD_DIM, HALF), F32)
-            for h in range(HEADS):
-                part = mixed[c, half, h * HEAD_DIM : (h + 1) * HEAD_DIM]
-                square = square + part * part
-            mean = jnp.sum(square, axis=0, keepdims=True) * (1.0 / WIDTH)
-            scale = lax.rsqrt(mean + 1e-05)
-            for g in range(WIDTH // HALF):
-                at = slice(g * HALF, (g + 1) * HALF)
-                normed = (mixed[c, half, at] * scale * gain_col[at]).astype(BF16)
-                tokens = pl.ds(pl.multiple_of(c * STRETCH, STRETCH) + half * HALF, HALF)
-                out_ref[tokens, at] = normed.T
         return 0
 
-    lax.fori_loop(0, PIECES, finish, 0)
+    lax.fori_loop(0, bits, add_bucket, 0)
+
+    def tokens_out(b):
+        return pltpu.make_async_copy(out_ref.at[b], out_hbm.at[b], out_sem.at[b])
+
+    for b in range(TOKENS // HALF):
+        c, half = b // 2, b % 2
+        square = jnp.zeros((HEAD_DIM, HALF), F32)
+        for h in range(HEADS):
+            part = mixed[c, half, h * HEAD_DIM : (h + 1) * HEAD_DIM]
+            square = square + part * part
+        mean = jnp.sum(square, axis=0, keepdims=True) * (1.0 / WIDTH)
+        scale = lax.rsqrt(mean + 1e-05)
+        out_ref[b] = (mixed[c, half] * scale * gain_col[...]).astype(BF16)
+        tokens_out(b).start()
 
     @pl.when(me < SHARDS - 1)
     def _():
@@ -442,16 +447,19 @@
                     device_id={"ctx": lax.rem(me + 1, SHARDS)},
                 ).wait_send()
 
+    for b in range(TOKENS // HALF):
+        tokens_out(b).wait()
+
 
 def per_device(mixer_input, conv_weight, log_decay, level_weight, norm_gain):
-    vmem = pl.BlockSpec(memory_space=pltpu.VMEM)
     hbm = pl.BlockSpec(memory_space=pltpu.HBM)
-    return pl.pallas_call(
+    blocks = pl.pallas_call(
         kernel,
-        out_shape=jax.ShapeDtypeStruct((TOKENS, WIDTH), BF16),
+        out_shape=jax.ShapeDtypeStruct((TOKENS // HALF, WIDTH, HALF), BF16),
         in_specs=[hbm] * 5,
-        out_specs=vmem,
+        out_specs=hbm,
         scratch_shapes=[
+            pltpu.VMEM((TOKENS // HALF, WIDTH, HALF), BF16),
             pltpu.VMEM((TOKENS, WIDTH + 2 * STATE), BF16),
             pltpu.VMEM((4, WIDTH + 2 * STATE), F32),
             pltpu.VMEM((HEADS, TOKENS), F32),
@@ -476,6 +484,7 @@
             pltpu.VMEM((BITS, GROUP, ROWS, STATE), BF16),
             pltpu.SemaphoreType.DMA((4,)),
             pltpu.SemaphoreType.DMA((PIECES + 1,)),
+            pltpu.SemaphoreType.DMA((TOKENS // HALF,)),
             pltpu.SemaphoreType.DMA((2,)),
             pltpu.SemaphoreType.DMA,
             pltpu.SemaphoreType.DMA,
@@ -489,6 +498,7 @@
             collective_id=0, has_side_effects=True, vmem_limit_bytes=63 << 20
         ),
     )(mixer_input, conv_weight, log_decay, level_weight, norm_gain.reshape(1, WIDTH))
+    return blocks.transpose(0, 2, 1).reshape(TOKENS, WIDTH)
 
 
 def solution(mesh):

time: 35.2 us -> 31 us (0.88)
  the two profiles are of different devices: /device:TPU:252 before, /device:TPU:2 now
where the time goes in v3:
time: 31 us; the launch traced here: 30.4 us
  Pallas kernels  28.2 us (91%)
  local copies, waits for them, and re-layouts  2.27 us (7%)
    pallas_call x1, Pallas kernels, per_device(): pl.pallas_call(kernel, out_shape=jax.ShapeDtypeStruct((TOKENS // HALF, WI...  28.2 us
    transpose x1, local copies, waits for them, and re-layouts, per_device(): return blocks.transpose(0, 2, 1).reshape(TOKENS, WIDTH)  2.27 us

profile of v3, /device:TPU:2, one launch (start us, length us, event | category | flops | bytes accessed | tf_op | source)
XLA Modules:
  0.0 30.4 jit_solution(12333933043499590920)
XLA Ops:
  0.0 28.2 %shard_map.55 = bf16[8,512,128]{2,1,0:T(8,128)(2,1)} custom-call(bf16[1024,768]{1,0:T(8,128)(2,1)} %x_hbm.1, f32[4,768]{1,0:T(4,128)} %conv_hbm.1, f32[8,1024]{1,0:T(8,128)} %rate_hbm.1, f32[7,8,1024]{2,1,0:T(8,128)} %level_hbm.1, f32[1,512]{1,0:T(1,128)} %bitcast.4), custom_call_target="tpu_custom_call" | custom-call | tf_op jit(solution)/shard_map/pallas_call | solution.py:456
  28.2 2.3 %copy.6 = bf16[8,128,512]{2,1,0:T(8,128)(2,1)} copy(bf16[8,128,512]{1,2,0:T(8,128)(2,1)} %bitcast.3) | data formatting | bytes 2097152 | tf_op jit(solution)/shard_map/transpose | solution.py:501

commit v4 on v3

--- a/solution.py
+++ b/solution.py
@@ -17,6 +17,7 @@
 SHARDS = 32
 ALONG_Z = 8
 ALONG_Y = 4
+OFFSETS = (4, 3, 5, 2, 6, 1, 7, 0)
 BITS = 5
 HALF = 128
 GROUP = 16
@@ -55,6 +56,8 @@
     pair = me // GROUP
     place_in = lax.rem(me, GROUP)
     odd = lax.rem(me, 2)
+    place_z = lax.rem(me, ALONG_Z)
+    row_in = place_in // ALONG_Z
     middle = popcount(place_in // 2)
 
     barrier = pltpu.get_barrier_semaphore()
@@ -75,13 +78,9 @@
 
     head_in = rows_in(0, STRETCH - 16, 0)
     tail_in = rows_in(TOKENS - 16, 16, PIECES)
-    for copy in small_in[:3]:
-        copy.start()
+    small_in[0].start()
     tail_in.start()
-    for c in range(PIECES - 1, 0, -1):
-        stretch_in(c).start()
-    head_in.start()
-    small_in[3].start()
+    stretch_in(PIECES - 1).start()
 
     def greet(d, _):
         other = lax.rem(me + d, SHARDS)
@@ -89,6 +88,13 @@
         return 0
 
     lax.fori_loop(1, SHARDS, greet, 0)
+
+    small_in[1].start()
+    small_in[2].start()
+    for c in range(PIECES - 2, 0, -1):
+        stretch_in(c).start()
+    head_in.start()
+    small_in[3].start()
 
     small_in[0].wait()
     rows = lax.broadcasted_iota(jnp.int32, (STRETCH, STRETCH), 0)
@@ -137,7 +143,7 @@
         )
 
     to_next = pltpu.make_async_remote_copy(
-        src_ref=x_hbm.at[pl.ds(TOKENS - 16, 16)], dst_ref=halo,
+        src_ref=x_ref.at[pl.ds(TOKENS - 16, 16)], dst_ref=halo,
         send_sem=halo_sem.at[0], recv_sem=halo_sem.at[1],
         device_id={"ctx": lax.rem(me + 1, SHARDS)},
     )
@@ -222,15 +228,18 @@
             carried = fall * carried + state[c, at]
         send1[2 * h : 2 * (h + 1)] = carried.astype(BF16).reshape(2, ROWS, STATE)
 
-    def spread(d, _):
-        there = lax.rem(place_in + d, GROUP)
-        pltpu.make_async_remote_copy(
-            src_ref=send1.at[there], dst_ref=recv1.at[place_in],
-            send_sem=p1_send, recv_sem=p1_recv, device_id={"ctx": pair * GROUP + there},
-        ).start()
-        return 0
-
-    lax.fori_loop(1, GROUP, spread, 0)
+    def across(along, down):
+        return (row_in + down) % 2 * ALONG_Z + lax.rem(place_z + along, ALONG_Z)
+
+    for along in OFFSETS:
+        for down in (1, 0):
+            if along or down:
+                there = across(along, down)
+                pltpu.make_async_remote_copy(
+                    src_ref=send1.at[there], dst_ref=recv1.at[place_in],
+                    send_sem=p1_send, recv_sem=p1_recv, device_id={"ctx": pair * GROUP + there},
+                ).start()
+
     recv1[place_in] = send1[place_in]
 
     small_in[2].wait()
@@ -275,24 +284,24 @@
                     own = own + readout[at] * near_scale[h : h + 1]
                 mixed[c, half, at] = own
 
+    neighbour = pltpu.make_async_remote_copy(
+        src_ref=send1, dst_ref=recv3.at[pair],
+        send_sem=p0_sem.at[0], recv_sem=p0_sem.at[1],
+        device_id={"ctx": lax.rem(me + 1, SHARDS)},
+    )
+
+    @pl.when(odd == 0)
+    def _():
+        neighbour.start()
+
     small_in[3].wait()
     near_own(0, False)
     wait_bytes(spans, ALONG_Z - 1, span_sem.at[0], span_sem.at[1]).wait()
     for d in range(1, ALONG_Y):
         span_along_column(d).start()
 
-    neighbour = pltpu.make_async_remote_copy(
-        src_ref=send1, dst_ref=recv3.at[pair],
-        send_sem=p0_sem.at[0], recv_sem=p0_sem.at[1],
-        device_id={"ctx": lax.rem(me + 1, SHARDS)},
-    )
-
     def rest(c, _):
         near_own(c, True)
-
-        @pl.when((odd == 0) & (c == 1))
-        def _():
-            neighbour.start()
 
         return 0
 
@@ -315,10 +324,7 @@
         falls = [falls[i] + falls[i + 1] for i in range(0, len(falls), 2)]
     top[...] = ends[0].astype(BF16)
 
-    def answer(i, _):
-        early = jnp.where(i < 4, 1, 0)
-        turn = lax.rem(place_in + i, 4) * early + lax.rem(place_in + i, 12) * (1 - early)
-        there = early * ((turn // 2) * ALONG_Z + turn % 2) + (1 - early) * ((turn // 6) * ALONG_Z + 2 + turn % 6)
+    def answer(there):
         @pl.when(pair == 0)
         def _():
             pltpu.make_async_remote_copy(
@@ -339,9 +345,18 @@
                     device_id={"ctx": pair * GROUP + there},
                 ).start()
 
-        return 0
-
-    lax.fori_loop(0, GROUP, answer, 0)
+
+    for t in range(4):
+        turn = lax.rem(place_in + t, 4)
+        answer(turn // 2 * ALONG_Z + turn % 2)
+    for along in OFFSETS:
+        for down in (1, 0):
+            there = across(along, down)
+
+            @pl.when(lax.rem(there, ALONG_Z) >= 2)
+            def _(there=there):
+                answer(there)
+
     for n in range(1, MIDDLE + 1):
 
         @pl.when(middle == n)

time: 31 us -> 30.5 us (0.984)
  Pallas kernels: 28.2 us -> 27.6 us
    pallas_call x1, Pallas kernels: 28.2 us -> 27.6 us  [per_device(): pl.pallas_call(kernel, out_shape=jax.ShapeDtypeStruct((TOKENS // HALF, WI...]
where the time goes in v4:
time: 30.5 us; the launch traced here: 29.9 us
  Pallas kernels  27.6 us (90%)
  local copies, waits for them, and re-layouts  2.27 us (7%)
    pallas_call x1, Pallas kernels, per_device(): pl.pallas_call(kernel, out_shape=jax.ShapeDtypeStruct((TOKENS // HALF, WI...  27.6 us
    transpose x1, local copies, waits for them, and re-layouts, per_device(): return blocks.transpose(0, 2, 1).reshape(TOKENS, WIDTH)  2.27 us

profile of v4, /device:TPU:2, one launch (start us, length us, event | category | flops | bytes accessed | tf_op | source)
XLA Modules:
  0.0 29.9 jit_solution(11667985693764032560)
XLA Ops:
  0.0 27.6 %shard_map.55 = bf16[8,512,128]{2,1,0:T(8,128)(2,1)} custom-call(bf16[1024,768]{1,0:T(8,128)(2,1)} %x_hbm.1, f32[4,768]{1,0:T(4,128)} %conv_hbm.1, f32[8,1024]{1,0:T(8,128)} %rate_hbm.1, f32[7,8,1024]{2,1,0:T(8,128)} %level_hbm.1, f32[1,512]{1,0:T(1,128)} %bitcast.4), custom_call_target="tpu_custom_call" | custom-call | tf_op jit(solution)/shard_map/pallas_call | solution.py:471
  27.7 2.3 %copy.6 = bf16[8,128,512]{2,1,0:T(8,128)(2,1)} copy(bf16[8,128,512]{1,2,0:T(8,128)(2,1)} %bitcast.3) | data formatting | bytes 2097152 | tf_op jit(solution)/shard_map/transpose | solution.py:516

commit v5 on v4

--- a/solution.py
+++ b/solution.py
@@ -18,6 +18,7 @@
 ALONG_Z = 8
 ALONG_Y = 4
 OFFSETS = (4, 3, 5, 2, 6, 1, 7, 0)
+ANSWERS = (5, 6, 7, 4, 3, 2, 1, 0)
 BITS = 5
 HALF = 128
 GROUP = 16
@@ -232,7 +233,7 @@
         return (row_in + down) % 2 * ALONG_Z + lax.rem(place_z + along, ALONG_Z)
 
     for along in OFFSETS:
-        for down in (1, 0):
+        for down in (0, 1):
             if along or down:
                 there = across(along, down)
                 pltpu.make_async_remote_copy(
@@ -349,7 +350,7 @@
     for t in range(4):
         turn = lax.rem(place_in + t, 4)
         answer(turn // 2 * ALONG_Z + turn % 2)
-    for along in OFFSETS:
+    for along in ANSWERS:
         for down in (1, 0):
             there = across(along, down)
 

time: 30.5 us -> 29.9 us (0.980); the launches traced: 29.9 us -> 29.7 us
  no operation moved by 1% of the time
where the time goes in v5:
time: 29.9 us; the launch traced here: 29.7 us
  Pallas kernels  27.5 us (92%)
  local copies, waits for them, and re-layouts  2.27 us (8%)
    pallas_call x1, Pallas kernels, per_device(): pl.pallas_call(kernel, out_shape=jax.ShapeDtypeStruct((TOKENS // HALF, WI...  27.5 us
    transpose x1, local copies, waits for them, and re-layouts, per_device(): return blocks.transpose(0, 2, 1).reshape(TOKENS, WIDTH)  2.27 us

profile of v5, /device:TPU:2, one launch (start us, length us, event | category | flops | bytes accessed | tf_op | source)
XLA Modules:
  0.0 29.7 jit_solution(9024940951791944948)
XLA Ops:
  0.0 27.5 %shard_map.55 = bf16[8,512,128]{2,1,0:T(8,128)(2,1)} custom-call(bf16[1024,768]{1,0:T(8,128)(2,1)} %x_hbm.1, f32[4,768]{1,0:T(4,128)} %conv_hbm.1, f32[8,1024]{1,0:T(8,128)} %rate_hbm.1, f32[7,8,1024]{2,1,0:T(8,128)} %level_hbm.1, f32[1,512]{1,0:T(1,128)} %bitcast.4), custom_call_target="tpu_custom_call" | custom-call | tf_op jit(solution)/shard_map/pallas_call | solution.py:472
  27.5 2.3 %copy.6 = bf16[8,128,512]{2,1,0:T(8,128)(2,1)} copy(bf16[8,128,512]{1,2,0:T(8,128)(2,1)} %bitcast.3) | data formatting | bytes 2097152 | tf_op jit(solution)/shard_map/transpose | solution.py:517

commit v6 on v5

--- a/solution.py
+++ b/solution.py
@@ -18,7 +18,7 @@
 ALONG_Z = 8
 ALONG_Y = 4
 OFFSETS = (4, 3, 5, 2, 6, 1, 7, 0)
-ANSWERS = (5, 6, 7, 4, 3, 2, 1, 0)
+ANSWERS = (5, 3, 6, 2, 7, 4, 1, 0)
 BITS = 5
 HALF = 128
 GROUP = 16
@@ -251,10 +251,7 @@
             jnp.where(diag, row, 0.0), axis=1, keepdims=True
         )
     for c in range(PIECES):
-        rate = rate_ref[:, c * STRETCH : (c + 1) * STRETCH] * LOG2E
-        column[c] = lax.dot_general(
-            lower, rate, NT, precision=lax.Precision.HIGHEST, preferred_element_type=F32
-        )
+        column[c] = inner[c].T
     causal = (rows <= cols)[:HALF, :HALF]
 
     def near_own(c, before):

time: 29.9 us -> 29.6 us (0.990)
  Pallas kernels: 27.5 us -> 27.1 us
    pallas_call x1, Pallas kernels: 27.5 us -> 27.1 us  [per_device(): pl.pallas_call(kernel, out_shape=jax.ShapeDtypeStruct((TOKENS // HALF, WI...]
where the time goes in v6:
time: 29.6 us; the launch traced here: 29.4 us
  Pallas kernels  27.1 us (92%)
  local copies, waits for them, and re-layouts  2.27 us (8%)
    pallas_call x1, Pallas kernels, per_device(): pl.pallas_call(kernel, out_shape=jax.ShapeDtypeStruct((TOKENS // HALF, WI...  27.1 us
    transpose x1, local copies, waits for them, and re-layouts, per_device(): return blocks.transpose(0, 2, 1).reshape(TOKENS, WIDTH)  2.27 us

profile of v6, /device:TPU:2, one launch (start us, length us, event | category | flops | bytes accessed | tf_op | source)
XLA Modules:
  0.0 29.4 jit_solution(12823383446106561489)
XLA Ops:
  0.0 27.1 %shard_map.55 = bf16[8,512,128]{2,1,0:T(8,128)(2,1)} custom-call(bf16[1024,768]{1,0:T(8,128)(2,1)} %x_hbm.1, f32[4,768]{1,0:T(4,128)} %conv_hbm.1, f32[8,1024]{1,0:T(8,128)} %rate_hbm.1, f32[7,8,1024]{2,1,0:T(8,128)} %level_hbm.1, f32[1,512]{1,0:T(1,128)} %bitcast.4), custom_call_target="tpu_custom_call" | custom-call | tf_op jit(solution)/shard_map/pallas_call | solution.py:469
  27.1 2.3 %copy.6 = bf16[8,128,512]{2,1,0:T(8,128)(2,1)} copy(bf16[8,128,512]{1,2,0:T(8,128)(2,1)} %bitcast.3) | data formatting | bytes 2097152 | tf_op jit(solution)/shard_map/transpose | solution.py:514

commit v7 on v6

--- a/solution.py
+++ b/solution.py
@@ -347,20 +347,6 @@
     for t in range(4):
         turn = lax.rem(place_in + t, 4)
         answer(turn // 2 * ALONG_Z + turn % 2)
-    for along in ANSWERS:
-        for down in (1, 0):
-            there = across(along, down)
-
-            @pl.when(lax.rem(there, ALONG_Z) >= 2)
-            def _(there=there):
-                answer(there)
-
-    for n in range(1, MIDDLE + 1):
-
-        @pl.when(middle == n)
-        def _():
-            recv3[pl.ds(pair + odd, n), place_in] = stage[:n, place_in]
-
     for k in range(BITS):
         digit = (me // 2**k) % 2
         if k == 0:
@@ -386,6 +372,20 @@
                     slot_weight[2 * c + half, slot] = level_ref[2 + k, :, tokens] * jnp.exp2(
                         gap + inner[c, :, half * HALF : (half + 1) * HALF]
                     )
+
+    for along in ANSWERS:
+        for down in (1, 0):
+            there = across(along, down)
+
+            @pl.when(lax.rem(there, ALONG_Z) >= 2)
+            def _(there=there):
+                answer(there)
+
+    for n in range(1, MIDDLE + 1):
+
+        @pl.when(middle == n)
+        def _():
+            recv3[pl.ds(pair + odd, n), place_in] = stage[:n, place_in]
 
     def add_bucket(i, _):
         slot = lax.rem(pair + i, bits)

time: 29.6 us -> 29.8 us (level)
  no operation moved by 1% of the time
where the time goes in v7:
time: 29.8 us; the launch traced here: 29.5 us
  Pallas kernels  27.2 us (91%)
  local copies, waits for them, and re-layouts  2.27 us (8%)
    pallas_call x1, Pallas kernels, per_device(): pl.pallas_call(kernel, out_shape=jax.ShapeDtypeStruct((TOKENS // HALF, WI...  27.2 us
    transpose x1, local copies, waits for them, and re-layouts, per_device(): return blocks.transpose(0, 2, 1).reshape(TOKENS, WIDTH)  2.27 us

profile of v7, /device:TPU:2, one launch (start us, length us, event | category | flops | bytes accessed | tf_op | source)
XLA Modules:
  0.0 29.5 jit_solution(10395456251754317080)
XLA Ops:
  0.0 27.2 %shard_map.55 = bf16[8,512,128]{2,1,0:T(8,128)(2,1)} custom-call(bf16[1024,768]{1,0:T(8,128)(2,1)} %x_hbm.1, f32[4,768]{1,0:T(4,128)} %conv_hbm.1, f32[8,1024]{1,0:T(8,128)} %rate_hbm.1, f32[7,8,1024]{2,1,0:T(8,128)} %level_hbm.1, f32[1,512]{1,0:T(1,128)} %bitcast.4), custom_call_target="tpu_custom_call" | custom-call | tf_op jit(solution)/shard_map/pallas_call | solution.py:469
  27.2 2.3 %copy.6 = bf16[8,128,512]{2,1,0:T(8,128)(2,1)} copy(bf16[8,128,512]{1,2,0:T(8,128)(2,1)} %bitcast.3) | data formatting | bytes 2097152 | tf_op jit(solution)/shard_map/transpose | solution.py:514
